TPU v7x, 128 devices: a whole 4x4x4 slice. The times are simulated.
128 devices in a mesh: row: 8 (over x, core), col: 16 (over y, z).
Axes of the slice: x: 4, y: 4, z: 4, core: 2. Of those that a mesh axis runs over, the one named last changes fastest.
Arguments:
- left_tiles: bfloat16 [8192, 4096], P('row', 'col'), may hold values from -6 to 6
- right_tiles: bfloat16 [4096, 16384], P('row', 'col'), may hold values from -0.09375 to 0.09375
- left_mask: int32 [64, 32], P('row', 'col'), may hold values from 0 to 1, as said below
- right_mask: int32 [32, 128], P('row', 'col'), may hold values from 0 to 1, as said below
- cycle_weight: bfloat16 [16384, 1024], P('col', 'row'), may hold values from -0.046875 to 0.046875
Outputs:
- cycle_out: float32 [64, 128, 1024], P('row', 'col')
Inputs may be any that keep to these rules, and one draw needn't show every extreme that they name: `left_mask`: each tile row i keeps each of its tiles with chance one, two or three thirds, the level drawn per row. `right_mask`: each tile column a keeps each of its tiles with chance one, two or three thirds, the level drawn per column.
All inputs are finite; a program needn't handle non-finite values.
Results may differ from a plain program's by a relative error of at most 0.0029.
Values may be sent and summed in bfloat16 or wider, within the bound.
A program may use at most 64 MiB of HBM per device.

v0:
```python
import jax
import jax.numpy as jnp
from jax import lax
from jax.sharding import PartitionSpec as P

JOCC = 128
VIRT_B = 128


def apply_mask(tiles, mask):
    rows, cols = tiles.shape
    mrows, mcols = mask.shape
    shaped = tiles.reshape(mrows, rows // mrows, mcols, cols // mcols)
    return (shaped * mask[:, None, :, None].astype(tiles.dtype)).reshape(rows, cols)


def body(left_tiles, right_tiles, left_mask, right_mask, cycle_weight):
    masked_left = apply_mask(left_tiles, left_mask)
    masked_right = apply_mask(right_tiles, right_mask)
    gathered = lax.all_gather(masked_left, "col", axis=1, tiled=True)
    totals = jnp.dot(
        gathered,
        lax.all_gather(masked_right, "row", axis=0, tiled=True),
        preferred_element_type=jnp.float32,
    )
    occ_local = left_mask.shape[0]
    vir_local = right_mask.shape[1]
    pair_block = totals.astype(jnp.bfloat16).reshape(occ_local, JOCC, vir_local, VIRT_B)
    relaid = lax.all_to_all(pair_block, "col", split_axis=1, concat_axis=2, tiled=True)
    piece = lax.all_gather(cycle_weight, "row", axis=1, tiled=True)
    operand = piece.reshape(piece.shape[0] // VIRT_B, VIRT_B, piece.shape[1])
    cycle_terms = jnp.einsum("ijab,jbk->iak", relaid, operand, preferred_element_type=jnp.float32)
    return lax.psum_scatter(cycle_terms, "col", scatter_dimension=1, tiled=True)


def solution(mesh):
    placed = (P("row", "col"), P("row", "col"), P("row", "col"), P("row", "col"), P("col", "row"))
    return jax.shard_map(
        body, mesh=mesh, in_specs=placed, out_specs=P("row", "col", None), check_vma=False
    )
```

profile of v0, /device:TPU:0, one launch (start us, length us, event | category | flops | bytes accessed | tf_op | source)
XLA Modules:
  0.0 281.0 jit_solution(11570222039503494329)
XLA Ops:
  6.5 0.0 all-gather.6.cloned.1.call-start
  6.5 0.7 convert_element_type.12
  7.2 0.2 mul.25
  7.4 0.0 copy-start.1
  7.4 0.0 copy-start
  7.5 2.4 bitcast_multiply_fusion
  9.9 0.0 all-gather.6.cloned.1.call-update
  9.9 0.0 all-gather.4.cloned.1.call-start
  9.9 0.0 copy-done.1
  9.9 0.1 copy.8
  10.0 0.3 mul.22
  10.4 0.0 copy-done
  10.4 0.9 bitcast_multiply_fusion.1
  11.3 0.0 all-gather.4.cloned.1.call-update
  11.3 0.0 all-gather.8.cloned.1.call-start
  11.4 0.7 all-gather.8.cloned.1.call-update
  12.0 50.1 %all-gather.6.cloned.1.call-done = bf16[4096,1024]{1,0:T(8,128)(2,1)} async-done(((bf16[512,1024]{1,0:T(8,128)(2,1)}), bf16[4096,1024]{1,0:T(8,128)(2,1)}) %all-gather.6.cloned.1.call-update) | async-done | bytes 8388624 | tf_op jit(solution)/shard_map/all_gather | solution.py:23
  62.2 80.9 %all-gather.4.cloned.1.call-done = bf16[1024,4096]{1,0:T(8,128)(2,1)} async-done(((bf16[1024,256]{1,0:T(8,128)(2,1)}), bf16[1024,4096]{1,0:T(8,128)(2,1)}) %all-gather.4.cloned.1.call-update) | async-done | bytes 8388624 | tf_op jit(solution)/shard_map/all_gather | solution.py:20
  143.0 13.7 %convert_bitcast_fusion = bf16[128,8,8,128]{3,1,2,0:T(8,128)(2,1)S(1)} fusion(bf16[1024,4096]{1,0:T(8,128)(2,1)} %all-gather.4.cloned.1.call-done, bf16[4096,1024]{1,0:T(8,128)(2,1)} %all-gather.6.cloned.1.call-done), kind=kOutput, calls=%fused_computation.3 | convolution fusion | flops 8590983168 | bytes 18874368 | tf_op jit(solution)/shard_map/dot_general | solution.py:21
  156.7 0.6 copy.14
  157.3 1.9 copy.9
  159.3 4.9 %all-to-all-start = ((bf16[8,128,8,128]{3,2,0,1:T(8,128)(2,1)}), bf16[8,128,8,128]{3,2,0,1:T(8,128)(2,1)S(1)}, u32[]{:S(2)}, u32[]{:S(2)}) async-start(bf16[8,128,8,128]{3,2,0,1:T(8,128)(2,1)} %copy.9), calls=%async_computation | async-start | bytes 4194304 | tf_op jit(solution)/shard_map/all_to_all | solution.py:29
  164.2 0.0 reduce-scatter.2.cloned.1.call-start
  164.3 6.9 %all-gather.8.cloned.1.call-done = bf16[1024,1024]{1,0:T(8,128)(2,1)} async-done(((bf16[1024,128]{1,0:T(8,128)(2,1)}), bf16[1024,1024]{1,0:T(8,128)(2,1)}) %all-gather.8.cloned.1.call-update) | async-done | bytes 2097168 | tf_op jit(solution)/shard_map/all_gather | solution.py:30
  171.2 21.9 %all-to-all-done = bf16[8,128,8,128]{3,2,0,1:T(8,128)(2,1)S(1)} async-done(((bf16[8,128,8,128]{3,2,0,1:T(8,128)(2,1)}), bf16[8,128,8,128]{3,2,0,1:T(8,128)(2,1)S(1)}, u32[]{:S(2)}, u32[]{:S(2)}) %all-to-all-start) | async-done | bytes 2097184 | tf_op jit(solution)/shard_map/all_to_all | solution.py:29
  193.1 5.4 %convolution_bitcast_fusion = f32[8,128,1024]{2,1,0:T(8,128)} fusion(bf16[8,128,1024,1]{2,1,0,3:T(8,128)(2,1)} %bitcast.31, bf16[8,16,8,8,128]{4,3,0,2,1:T(8,128)(2,1)S(1)} %bitcast.30), kind=kOutput, calls=%fused_computation | convolution fusion | flops 2147483648 | bytes 8388608 | tf_op jit(solution)/shard_map/ijab,jbk->iak/dot_general | solution.py:32
  198.5 0.0 reduce-scatter.2.cloned.1.call-update
  198.5 75.9 %reduce-scatter.2.cloned.1.call-done = f32[8,8,1024]{2,1,0:T(8,128)} async-done(((f32[8,128,1024]{2,1,0:T(8,128)}), f32[8,8,1024]{2,1,0:T(8,128)}) %reduce-scatter.2.cloned.1.call-update) | async-done | bytes 262160 | tf_op jit(solution)/shard_map/reduce_scatter | solution.py:33
  (1 shorter events, 0.0 us)
Async XLA Ops:
  6.5 55.6 %all-gather.6.cloned.1.call-start = ((), (), s32[]{:S(2)}) async-start(), calls=%async_computation.3 | async-start | bytes 9437184 | tf_op jit(solution)/shard_map/all_gather | solution.py:23
  7.4 2.5 copy-start.1
  7.4 2.9 %copy-start = (bf16[1024,256]{1,0:T(8,128)(2,1)S(1)}, bf16[1024,256]{1,0:T(8,128)(2,1)}, u32[]{:S(2)}) copy-start(bf16[1024,256]{1,0:T(8,128)(2,1)} %param.5) | copy-start | bytes 1572868
  9.9 133.2 %all-gather.4.cloned.1.call-start = ((), (), s32[]{:S(2)}) async-start(), calls=%async_computation.2 | async-start | bytes 8912896 | tf_op jit(solution)/shard_map/all_gather | solution.py:20
  11.3 159.9 %all-gather.8.cloned.1.call-start = ((), (), s32[]{:S(2)}) async-start(), calls=%async_computation.4 | async-start | bytes 2359296 | tf_op jit(solution)/shard_map/all_gather | solution.py:30
  159.3 33.8 %all-to-all-start = ((bf16[8,128,8,128]{3,2,0,1:T(8,128)(2,1)}), bf16[8,128,8,128]{3,2,0,1:T(8,128)(2,1)S(1)}, u32[]{:S(2)}, u32[]{:S(2)}) async-start(bf16[8,128,8,128]{3,2,0,1:T(8,128)(2,1)} %copy.9), calls=%async_computation | async-start | bytes 4194304 | tf_op jit(solution)/shard_map/all_to_all | solution.py:29
  164.2 110.3 %reduce-scatter.2.cloned.1.call-start = ((), (), s32[]{:S(2)}) async-start(), calls=%async_computation.5 | async-start | bytes 4456448 | tf_op jit(solution)/shard_map/reduce_scatter | solution.py:33
Sparse Core Ops, SparseCore 0:
  10.0 52.1 all-gather.5
  64.3 78.7 all-gather.3
  144.7 26.4 all-gather.7
  198.7 75.7 reduce-scatter.1
where the time goes:
time: 281 us
  waiting for transfers between devices  236 us (84%)
  matrix products  19.1 us (7%)
  between operations  13.2 us (5%)
  starting transfers between devices  5.07 us (2%)
  other arithmetic  3.97 us (1%)
  local copies, waits for them, and re-layouts  3.2 us (1%)
    all_gather x1, waiting for transfers between devices, body(): gathered = lax.all_gather(masked_left, 'col', axis=1, tiled=True)  80.9 us
    reduce_scatter x1, waiting for transfers between devices, body(): return lax.psum_scatter(cycle_terms, 'col', scatter_dimension=1, tiled=True)  75.9 us
    all_gather x1, waiting for transfers between devices, body(): lax.all_gather(masked_right, 'row', axis=0, tiled=True)  50.1 us
    all_to_all x1, waiting for transfers between devices, body(): lax.all_to_all(pair_block, 'col', split_axis=1, concat_axis=2, tiled=True)  21.9 us
    dot_general x1, matrix products, body(): jnp.dot(gathered, lax.all_gather(masked_right, 'row', axis=0, tiled=True)...  13.7 us
    all_gather x1, waiting for transfers between devices, body(): piece = lax.all_gather(cycle_weight, 'row', axis=1, tiled=True)  6.95 us
  transfers between devices with their start and end apart: 5, of which 5 were waited for; matrix products, arithmetic and copies ran while one was open for 6% of the time, Pallas kernels for 0%

commit v1 on v0

--- a/solution.py
+++ b/solution.py
@@ -27,7 +27,9 @@
     vir_local = right_mask.shape[1]
     pair_block = totals.astype(jnp.bfloat16).reshape(occ_local, JOCC, vir_local, VIRT_B)
     relaid = lax.all_to_all(pair_block, "col", split_axis=1, concat_axis=2, tiled=True)
-    piece = lax.all_gather(cycle_weight, "row", axis=1, tiled=True)
+    piece = jnp.concatenate(
+        lax.all_to_all(jnp.stack([cycle_weight] * lax.axis_size("row")), "row", 0, 0), axis=1
+    )
     operand = piece.reshape(piece.shape[0] // VIRT_B, VIRT_B, piece.shape[1])
     cycle_terms = jnp.einsum("ijab,jbk->iak", relaid, operand, preferred_element_type=jnp.float32)
     return lax.psum_scatter(cycle_terms, "col", scatter_dimension=1, tiled=True)

time: 281 us -> 300 us (1.068)
  local copies, waits for them, and re-layouts: 3.2 us -> 10.3 us
  waiting for transfers between devices: 236 us -> 243 us
  starting transfers between devices: 5.07 us -> 9.46 us
    all_gather x1, waiting for transfers between devices: 50.1 us -> 62.5 us  [body(): lax.all_gather(masked_right, 'row', axis=0, tiled=True)]
    all_gather x1 -> x0, waiting for transfers between devices: 6.95 us -> none  [body(): piece = lax.all_gather(cycle_weight, 'row', axis=1, tiled=True)]
    another operation x0 -> x2, local copies, waits for them, and re-layouts: none -> 4.41 us  [the longest x1 2.82 us: body(): operand = piece.reshape(piece.shape[0] // VIRT_B, VIRT_B, piece.shape[1])]
    all_to_all x0 -> x1, starting transfers between devices: none -> 4.38 us  [body(): lax.all_to_all(jnp.stack([cycle_weight] * lax.axis_size('row')), 'row', 0...]
  transfers between devices with their start and end apart: 5 -> 5, of which waited for: 5 -> 4; matrix products, arithmetic and copies ran while one was open for 6% -> 8% of each run, Pallas kernels for 0% -> 0%
where the time goes in v1:
time: 300 us; the launch traced here: 299 us
  waiting for transfers between devices  243 us (81%)
  matrix products  19.1 us (6%)
  between operations  13.2 us (4%)
  local copies, waits for them, and re-layouts  10.3 us (3%)
  starting transfers between devices  9.46 us (3%)
  other arithmetic  3.97 us (1%)
    all_gather x1, waiting for transfers between devices, body(): gathered = lax.all_gather(masked_left, 'col', axis=1, tiled=True)  81.3 us
    reduce_scatter x1, waiting for transfers between devices, body(): return lax.psum_scatter(cycle_terms, 'col', scatter_dimension=1, tiled=True)  76 us
    all_gather x1, waiting for transfers between devices, body(): lax.all_gather(masked_right, 'row', axis=0, tiled=True)  62.5 us
    all_to_all x1, waiting for transfers between devices, body(): lax.all_to_all(pair_block, 'col', split_axis=1, concat_axis=2, tiled=True)  23.4 us
    dot_general x1, matrix products, body(): jnp.dot(gathered, lax.all_gather(masked_right, 'row', axis=0, tiled=True)...  13.7 us
  transfers between devices with their start and end apart: 5, of which 4 were waited for; matrix products, arithmetic and copies ran while one was open for 8% of the time, Pallas kernels for 0%

profile of v1, /device:TPU:0, one launch (start us, length us, event | category | flops | bytes accessed | tf_op | source)
XLA Modules:
  0.0 299.3 jit_solution(7338317515574909082)
XLA Ops:
  6.5 0.0 all-gather.5.cloned.1.call-start
  6.5 0.7 convert_element_type.12
  7.2 0.2 mul.25
  7.4 0.0 copy-start.2
  7.4 0.0 copy-start
  7.5 2.4 bitcast_multiply_fusion
  9.9 0.0 copy-start.1
  9.9 0.0 all-gather.5.cloned.1.call-update
  9.9 0.0 all-gather.3.cloned.1.call-start
  9.9 0.0 copy-done.2
  9.9 0.1 copy.8
  10.0 0.3 mul.22
  10.4 0.0 copy-done
  10.4 0.9 bitcast_multiply_fusion.1
  11.3 0.0 all-gather.3.cloned.1.call-update
  11.3 0.0 copy-done.1
  11.3 1.6 stack.2
  12.9 4.4 %all-to-all-start.1 = ((bf16[8,1024,128]{2,1,0:T(8,128)(2,1)}), bf16[8,1024,128]{2,1,0:T(8,128)(2,1)S(1)}, u32[]{:S(2)}, u32[]{:S(2)}) async-start(bf16[8,1024,128]{2,1,0:T(8,128)(2,1)} %stack.2), calls=%async_computation.1 | async-start | bytes 4194304 | tf_op jit(solution)/shard_map/all_to_all | solution.py:31
  17.3 62.5 %all-gather.5.cloned.1.call-done = bf16[4096,1024]{1,0:T(8,128)(2,1)} async-done(((bf16[512,1024]{1,0:T(8,128)(2,1)}), bf16[4096,1024]{1,0:T(8,128)(2,1)}) %all-gather.5.cloned.1.call-update) | async-done | bytes 8388624 | tf_op jit(solution)/shard_map/all_gather | solution.py:23
  79.8 81.3 %all-gather.3.cloned.1.call-done = bf16[1024,4096]{1,0:T(8,128)(2,1)} async-done(((bf16[1024,256]{1,0:T(8,128)(2,1)}), bf16[1024,4096]{1,0:T(8,128)(2,1)}) %all-gather.3.cloned.1.call-update) | async-done | bytes 8388624 | tf_op jit(solution)/shard_map/all_gather | solution.py:20
  161.1 13.7 %convert_bitcast_fusion = bf16[128,8,8,128]{3,1,2,0:T(8,128)(2,1)S(1)} fusion(bf16[1024,4096]{1,0:T(8,128)(2,1)} %all-gather.3.cloned.1.call-done, bf16[4096,1024]{1,0:T(8,128)(2,1)} %all-gather.5.cloned.1.call-done), kind=kOutput, calls=%fused_computation.3 | convolution fusion | flops 8590983168 | bytes 18874368 | tf_op jit(solution)/shard_map/dot_general | solution.py:21
  174.7 0.6 copy.15
  175.4 1.9 copy.9
  177.3 0.0 all-to-all-done.1
  177.3 5.0 %all-to-all-start = ((bf16[8,128,8,128]{3,2,0,1:T(8,128)(2,1)}), bf16[8,128,8,128]{3,2,0,1:T(8,128)(2,1)}, u32[]{:S(2)}, u32[]{:S(2)}) async-start(bf16[8,128,8,128]{3,2,0,1:T(8,128)(2,1)} %copy.9), calls=%async_computation | async-start | bytes 4194304 | tf_op jit(solution)/shard_map/all_to_all | solution.py:29
  182.3 0.0 reduce-scatter.2.cloned.1.call-start
  182.4 2.7 copy.11
  185.0 2.8 reshape.20
  187.8 23.4 %all-to-all-done = bf16[8,128,8,128]{3,2,0,1:T(8,128)(2,1)} async-done(((bf16[8,128,8,128]{3,2,0,1:T(8,128)(2,1)}), bf16[8,128,8,128]{3,2,0,1:T(8,128)(2,1)}, u32[]{:S(2)}, u32[]{:S(2)}) %all-to-all-start) | async-done | bytes 2097184 | tf_op jit(solution)/shard_map/all_to_all | solution.py:29
  211.2 5.5 %convolution_bitcast_fusion = f32[8,128,1024]{2,1,0:T(8,128)} fusion(bf16[8,128,1024,1]{2,1,0,3:T(8,128)(2,1)S(1)} %reshape.20, bf16[8,16,8,8,128]{4,3,0,2,1:T(8,128)(2,1)} %bitcast), kind=kOutput, calls=%fused_computation | convolution fusion | flops 2147483648 | bytes 8388608 | tf_op jit(solution)/shard_map/ijab,jbk->iak/dot_general | solution.py:34
  216.7 0.0 reduce-scatter.2.cloned.1.call-update
  216.7 76.0 %reduce-scatter.2.cloned.1.call-done = f32[8,8,1024]{2,1,0:T(8,128)} async-done(((f32[8,128,1024]{2,1,0:T(8,128)}), f32[8,8,1024]{2,1,0:T(8,128)}) %reduce-scatter.2.cloned.1.call-update) | async-done | bytes 262160 | tf_op jit(solution)/shard_map/reduce_scatter | solution.py:35
  (1 shorter events, 0.0 us)
Async XLA Ops:
  6.5 73.2 %all-gather.5.cloned.1.call-start = ((), (), s32[]{:S(2)}) async-start(), calls=%async_computation.4 | async-start | bytes 9437184 | tf_op jit(solution)/shard_map/all_gather | solution.py:23
  7.4 2.5 copy-start.2
  7.4 2.9 copy-start
  9.9 1.5 copy-start.1
  9.9 151.2 %all-gather.3.cloned.1.call-start = ((), (), s32[]{:S(2)}) async-start(), calls=%async_computation.3 | async-start | bytes 8912896 | tf_op jit(solution)/shard_map/all_gather | solution.py:20
  12.9 164.4 %all-to-all-start.1 = ((bf16[8,1024,128]{2,1,0:T(8,128)(2,1)}), bf16[8,1024,128]{2,1,0:T(8,128)(2,1)S(1)}, u32[]{:S(2)}, u32[]{:S(2)}) async-start(bf16[8,1024,128]{2,1,0:T(8,128)(2,1)} %stack.2), calls=%async_computation.1 | async-start | bytes 4194304 | tf_op jit(solution)/shard_map/all_to_all | solution.py:31
  177.3 33.9 %all-to-all-start = ((bf16[8,128,8,128]{3,2,0,1:T(8,128)(2,1)}), bf16[8,128,8,128]{3,2,0,1:T(8,128)(2,1)}, u32[]{:S(2)}, u32[]{:S(2)}) async-start(bf16[8,128,8,128]{3,2,0,1:T(8,128)(2,1)} %copy.9), calls=%async_computation | async-start | bytes 4194304 | tf_op jit(solution)/shard_map/all_to_all | solution.py:29
  182.3 110.5 %reduce-scatter.2.cloned.1.call-start = ((), (), s32[]{:S(2)}) async-start(), calls=%async_computation.5 | async-start | bytes 4456448 | tf_op jit(solution)/shard_map/reduce_scatter | solution.py:35
Sparse Core Ops, SparseCore 0:
  10.0 69.7 all-gather.4
  81.9 79.1 all-gather.2
  216.8 75.8 reduce-scatter.1
